TPU v7x, 32 devices: a whole 2x2x4 slice. The times are simulated.
32 devices in a mesh: groups: 2 (over y), dp: 2 (over core), tensor: 8 (over z, x).
Axes of the slice: x: 2, y: 2, z: 4, core: 2. Of those that a mesh axis runs over, the one named last changes fastest.
Arguments:
- activations: bfloat16 [2048, 14336], P(('groups', 'dp'), 'tensor'), parts along dimension 0, may hold values from -6 to 6
- base_weight: bfloat16 [14336, 8192], P('tensor'), may hold values from -0.046875 to 0.046875
- adapter_down: bfloat16 [32, 16, 14336], P(('groups', 'tensor')), parts along dimension 0, may hold values from -0.046875 to 0.046875
- adapter_up: bfloat16 [32, 16, 8192], P(('groups', 'tensor')), parts along dimension 0, may hold values from -1.5 to 1.5
- block_adapter: int32 [4, 64], P(('groups', 'dp')), parts along dimension 0, may hold values from 0 to 15, as said below
- block_live: int32 [4, 64], P(('groups', 'dp')), parts along dimension 0, may hold values from 1 to 8, 320 in all within a row
- cotangent: bfloat16 [2048, 8192], P(('groups', 'dp'), 'tensor'), parts along dimension 0, may hold values from -6 to 6
Outputs:
- layer_out: bfloat16 [2048, 8192], P(('groups', 'dp'), 'tensor'), parts along dimension 0
- grad_input: bfloat16 [2048, 14336], P(('groups', 'dp'), 'tensor'), parts along dimension 0
- grad_down: bfloat16 [32, 16, 14336], P(('groups', 'tensor')), parts along dimension 0
- grad_up: bfloat16 [32, 16, 8192], P(('groups', 'tensor')), parts along dimension 0
There are 2 independent parts, one for each index of `groups`. A program takes and returns all parts, laid end to end along the dimension named above; an argument that names none is the same for every part. Nothing has to cross between parts.
Inputs may be any that keep to these rules, and one draw needn't show every extreme that they name: `block_adapter`: index t of tensor owns the adapters t * 2 to (t + 1) * 2 - 1; in each row group the adapters of every owner name exactly 8 blocks. `block_live`: in each row group the entries add up to 320.
All inputs are finite; a program needn't handle non-finite values.
Results may differ from a plain program's by a relative error of at most 0.0051.
Values may be sent and summed in bfloat16 or wider, within the bound.
A program may use at most 256 MiB of HBM per device.

v0:
```python
import jax
import jax.numpy as jnp
from jax import lax
from jax.sharding import PartitionSpec as P

lowrank_scale = 0.5


def body(activations, base_weight, adapter_down, adapter_up, block_adapter, block_live, cotangent):
    tensor_count = lax.axis_size("tensor")
    own_index = lax.axis_index("tensor")
    row_count, ff_dev = activations.shape
    d_dev = cotangent.shape[1]
    own_count = adapter_down.shape[0]
    block_ids = block_adapter.reshape(-1)
    block_count = block_ids.shape[0]
    block_rows = row_count // block_count
    per_owner = block_count // tensor_count
    owner_of = block_ids // own_count
    block_iota = jnp.arange(block_count, dtype=jnp.int32)
    same_owner = owner_of[:, None] == owner_of[None, :]
    before = block_iota[None, :] < block_iota[:, None]
    position = jnp.sum((same_owner & before).astype(jnp.int32), axis=1)
    slot_of_block = owner_of * per_owner + position
    row_iota = jnp.arange(block_rows, dtype=jnp.int32)
    live = (row_iota[None, :] < block_live.reshape(-1)[:, None]).astype(jnp.float32)
    live_rows = live.reshape(row_count, 1)
    slot_iota = jnp.arange(per_owner, dtype=jnp.int32)
    owned_here = owner_of == own_index
    slot_pick = owned_here[None, :] & (position[None, :] == slot_iota[:, None])
    local_ids = (
        jnp.sum(slot_pick.astype(jnp.int32) * block_ids[None, :], axis=1) - own_index * own_count
    )
    down_send = jnp.take(adapter_down, local_ids, axis=0)
    up_send = jnp.take(adapter_up, local_ids, axis=0)
    down_recv, up_recv = (
        lax.all_to_all(down_send, "tensor", split_axis=2, concat_axis=0, tiled=True),
        lax.all_to_all(up_send, "tensor", split_axis=2, concat_axis=0, tiled=True),
    )
    down_blocks = jnp.take(down_recv, slot_of_block, axis=0)
    up_block_list = jnp.take(up_recv, slot_of_block, axis=0)
    act_blocks = activations.reshape(block_count, block_rows, ff_dev)
    masked = cotangent * live_rows.astype(jnp.bfloat16)
    gradient_block_list = masked.reshape(block_count, block_rows, d_dev)
    low_part = jnp.einsum(
        "brf,bkf->brk", act_blocks, down_blocks, preferred_element_type=jnp.float32
    )
    back_part = jnp.einsum(
        "gys,gms->gym", gradient_block_list, up_block_list, preferred_element_type=jnp.float32
    )
    low_sum, back_sum = lax.psum((low_part, back_part), "tensor")
    rank_activations = low_sum.astype(jnp.bfloat16)
    rank_grads = (lowrank_scale * back_sum).astype(jnp.bfloat16)
    weight_cols = base_weight
    base_feat = lax.psum_scatter(
        lax.dot_general(
            weight_cols, activations, (((0,), (1,)), ((), ())), preferred_element_type=jnp.float32
        ),
        "tensor",
        scatter_dimension=0,
        tiled=True,
    )
    base_rows = base_feat.T
    weight_cols = base_weight
    through_base = lax.dot_general(
        lax.all_gather(masked, "tensor", axis=1, tiled=True),
        weight_cols,
        (((1,), (1,)), ((), ())),
        preferred_element_type=jnp.float32,
    )
    adapter_output = jnp.einsum(
        "nex,nxt->net", rank_activations, up_block_list, preferred_element_type=jnp.float32
    ).reshape(row_count, d_dev)
    layer_out = (live_rows * (base_rows + lowrank_scale * adapter_output)).astype(jnp.bfloat16)
    through_adapter = jnp.einsum(
        "brk,bkf->brf", rank_grads, down_blocks, preferred_element_type=jnp.float32
    ).reshape(row_count, ff_dev)
    grad_input = (through_base + through_adapter).astype(jnp.bfloat16)
    down_terms = jnp.einsum(
        "brk,brf->bkf", rank_grads, act_blocks, preferred_element_type=jnp.float32
    )
    up_projection_terms = lowrank_scale * jnp.einsum(
        "svu,svj->suj", rank_activations, gradient_block_list, preferred_element_type=jnp.float32
    )
    block_of_slot = jnp.zeros((block_count,), jnp.int32).at[slot_of_block].set(block_iota)
    down_slots = jnp.take(down_terms, block_of_slot, axis=0)
    up_slots = jnp.take(up_projection_terms, block_of_slot, axis=0)
    down_home, up_home = (
        lax.all_to_all(down_slots, "tensor", split_axis=0, concat_axis=2, tiled=True),
        lax.all_to_all(up_slots, "tensor", split_axis=0, concat_axis=2, tiled=True),
    )
    selector = (local_ids[:, None] == jnp.arange(own_count, dtype=jnp.int32)[None, :]).astype(
        jnp.float32
    )
    down_own = jnp.einsum("jl,jkf->lkf", selector, down_home, precision=lax.Precision.HIGHEST)
    up_own = jnp.einsum("jl,jkd->lkd", selector, up_home, precision=lax.Precision.HIGHEST)
    down_own, up_own = lax.psum((down_own, up_own), "dp")
    return (layer_out, grad_input, down_own.astype(jnp.bfloat16), up_own.astype(jnp.bfloat16))


def solution(mesh):
    in_specs = (
        P(("groups", "dp"), "tensor"),
        P("tensor", None),
        P(("groups", "tensor"), None, None),
        P(("groups", "tensor"), None, None),
        P(("groups", "dp"), None),
        P(("groups", "dp"), None),
        P(("groups", "dp"), "tensor"),
    )
    out_specs = (
        P(("groups", "dp"), "tensor"),
        P(("groups", "dp"), "tensor"),
        P(("groups", "tensor"), None, None),
        P(("groups", "tensor"), None, None),
    )
    return jax.shard_map(body, mesh=mesh, in_specs=in_specs, out_specs=out_specs, check_vma=False)
```

profile of v0, /device:TPU:28, one launch (start us, length us, event | category | flops | bytes accessed | tf_op | source)
XLA Modules:
  0.0 787.0 jit_solution(11652197044648916641)
XLA Ops:
  18.1 14.6 %copy.56 = bf16[8,16,8192]{1,0,2:T(8,128)(2,1)} copy(bf16[8,16,8192]{2,1,0:T(8,128)(2,1)} %broadcast_select_fusion.4) | data formatting | bytes 4194304 | tf_op jit(solution)/shard_map/jit(_take)/select_n | solution.py:35
  32.7 19.6 %reshape.258 = bf16[8,2,65536]{2,1,0:T(2,128)(2,1)} reshape(bf16[8192,8,16]{2,1,0:T(8,128)(2,1)} %bitcast.91) | data formatting | bytes 4194304
  52.3 6.0 all-to-all-start.1
  58.6 24.3 %fusion.34 = f32[8192,512]{1,0:T(8,128)} fusion(bf16[1792,8192]{1,0:T(8,128)(2,1)} %param.8, bf16[512,1792]{1,0:T(8,128)(2,1)S(1)} %copy-done), kind=kOutput, calls=%fused_computation.84 | convolution fusion | flops 15032385536 | bytes 47972352 | tf_op jit(solution)/shard_map/dot_general | solution.py:56
  86.6 4.3 broadcast_select_fusion.1
  90.9 24.0 %copy.53 = bf16[8,16,14336]{1,0,2:T(8,128)(2,1)} copy(bf16[8,16,14336]{2,1,0:T(8,128)(2,1)} %broadcast_select_fusion.1) | data formatting | bytes 7340032 | tf_op jit(solution)/shard_map/jit(_take)/select_n | solution.py:34
  114.9 33.6 %reshape.260 = bf16[8,2,114688]{2,1,0:T(2,128)(2,1)} reshape(bf16[14336,8,16]{2,1,0:T(8,128)(2,1)} %bitcast.89) | data formatting | bytes 7340032
  148.5 5.8 all-to-all-done.1
  154.4 12.1 %all-to-all-start = ((bf16[8,2,114688]{2,1,0:T(2,128)(2,1)}), bf16[8,2,114688]{2,1,0:T(2,128)(2,1)}, u32[]{:S(2)}, u32[]{:S(2)}) async-start(bf16[8,2,114688]{2,1,0:T(2,128)(2,1)} %reshape.260), calls=%async_computation.1 | async-start | bytes 7340032 | tf_op jit(solution)/shard_map/all_to_all | solution.py:37
  167.3 13.9 %reshape.259 = bf16[8192,8,16]{2,1,0:T(8,128)(2,1)} reshape(bf16[8,2,65536]{2,1,0:T(2,128)(2,1)} %all-to-all-done.1) | data formatting | bytes 4194304
  181.3 17.0 %copy.58 = bf16[8,8,16,1024]{3,2,1,0:T(8,128)(2,1)} copy(bf16[8,8,16,1024]{2,1,3,0:T(8,128)(2,1)} %bitcast.92) | data formatting | bytes 4194304 | tf_op jit(solution)/shard_map/all_to_all | solution.py:38
  198.3 3.7 gather_fusion.3
  204.5 93.4 %all-to-all-done = bf16[8,2,114688]{2,1,0:T(2,128)(2,1)} async-done(((bf16[8,2,114688]{2,1,0:T(2,128)(2,1)}), bf16[8,2,114688]{2,1,0:T(2,128)(2,1)}, u32[]{:S(2)}, u32[]{:S(2)}) %all-to-all-start) | async-done | bytes 3670048 | tf_op jit(solution)/shard_map/all_to_all | solution.py:37
  298.0 22.8 %reshape.261 = bf16[14336,8,16]{2,1,0:T(8,128)(2,1)} reshape(bf16[8,2,114688]{2,1,0:T(2,128)(2,1)} %all-to-all-done) | data formatting | bytes 7340032
  320.8 26.9 %copy.55 = bf16[8,8,16,1792]{3,2,1,0:T(8,128)(2,1)} copy(bf16[8,8,16,1792]{2,1,3,0:T(8,128)(2,1)} %bitcast.90) | data formatting | bytes 7340032 | tf_op jit(solution)/shard_map/all_to_all | solution.py:37
  347.7 4.8 gather_fusion.1
  352.5 4.4 fusion.7
  356.9 58.0 %all-reduce = (bf16[64,8,16]{2,1,0:T(8,128)(2,1)S(1)}, f32[64,8,16]{2,1,0:T(8,128)S(1)}) all-reduce(f32[64,8,16]{2,1,0:T(8,128)} %fusion.7, f32[64,8,16]{2,1,0:T(8,128)S(1)} %fusion.11), channel_id=1, replica_groups=mesh['groups'=2,'dp'=2,'tensor'=8] {'tensor'}, use_global_device_ids=true, to_apply=%region_3.4 | all-reduce | flops 16384 | bytes 114688 | tf_op jit(solution)/shard_map/psum | solution.py:51
  417.6 5.0 gather_fusion.5
  422.6 4.6 broadcast_select_fusion.3
  427.3 7.6 all-to-all-start.3
  438.5 7.1 gather_fusion.4
  445.6 7.0 broadcast_select_fusion
  452.6 99.3 %all-to-all-done.3 = f32[64,16,1024]{2,1,0:T(8,128)} async-done(((f32[64,16,1024]{2,1,0:T(8,128)}), f32[64,16,1024]{2,1,0:T(8,128)}, u32[]{:S(2)}, u32[]{:S(2)}) %all-to-all-start.3) | async-done | bytes 4194336 | tf_op jit(solution)/shard_map/all_to_all | solution.py:90
  551.9 12.4 %all-to-all-start.2 = ((f32[64,16,1792]{2,1,0:T(8,128)}), f32[64,16,1792]{2,1,0:T(8,128)}, u32[]{:S(2)}, u32[]{:S(2)}) async-start(f32[64,16,1792]{2,1,0:T(8,128)} %broadcast_select_fusion), calls=%async_computation.3 | async-start | bytes 14680064 | tf_op jit(solution)/shard_map/all_to_all | solution.py:89
  570.6 4.6 copy.61
  577.3 23.1 %fusion.35 = f32[512,1792]{1,0:T(8,128)} fusion(bf16[512,8192]{1,0:T(8,128)(2,1)} %all-gather.2.cloned.1.call-done, bf16[1792,8192]{1,0:T(8,128)(2,1)} %param.8), kind=kOutput, calls=%fused_computation.85 | convolution fusion | flops 15032385536 | bytes 41418752 | tf_op jit(solution)/shard_map/dot_general | solution.py:65
  600.5 4.3 fusion
  604.7 143.0 %all-to-all-done.2 = f32[64,16,1792]{2,1,0:T(8,128)} async-done(((f32[64,16,1792]{2,1,0:T(8,128)}), f32[64,16,1792]{2,1,0:T(8,128)}, u32[]{:S(2)}, u32[]{:S(2)}) %all-to-all-start.2) | async-done | bytes 7340064 | tf_op jit(solution)/shard_map/all_to_all | solution.py:89
  747.7 7.3 copy.60
  755.0 4.6 fusion.20
  759.7 11.7 %all-reduce.3 = (bf16[2,16,14336]{2,0,1:T(2,128)(2,1)}, bf16[2,16,8192]{2,0,1:T(2,128)(2,1)}) all-reduce(f32[2,16,14336]{2,0,1:T(2,128)} %fusion.20, f32[2,16,8192]{2,0,1:T(2,128)S(1)} %fusion.18), channel_id=1, replica_groups=mesh['groups'=2,'dp'=2,'tensor'=8] {'dp'}, use_global_device_ids=true, to_apply=%region_6.7 | all-reduce | flops 720896 | bytes 4325376 | tf_op jit(solution)/shard_map/psum | solution.py:97
  (56 shorter events, 41.5 us)
Async XLA Ops:
  7.2 51.4 %copy-start = (bf16[512,1792]{1,0:T(8,128)(2,1)S(1)}, bf16[512,1792]{1,0:T(8,128)(2,1)}, u32[]{:S(2)}) copy-start(bf16[512,1792]{1,0:T(8,128)(2,1)} %param.7) | copy-start | bytes 5505028
  7.2 5.8 copy-start.4
  7.2 570.1 %all-gather.2.cloned.1.call-start = ((), (), s32[]{:S(2)}) async-start(), calls=%async_computation.6 | async-start | bytes 9437184 | tf_op jit(solution)/shard_map/all_gather | solution.py:66
  8.2 6.7 copy-start.6
  52.3 102.1 %all-to-all-start.1 = ((bf16[8,2,65536]{2,1,0:T(2,128)(2,1)}), bf16[8,2,65536]{2,1,0:T(2,128)(2,1)}, u32[]{:S(2)}, u32[]{:S(2)}) async-start(bf16[8,2,65536]{2,1,0:T(2,128)(2,1)} %reshape.258), calls=%async_computation.2 | async-start | bytes 4194304 | tf_op jit(solution)/shard_map/all_to_all | solution.py:38
  58.3 717.5 %reduce-scatter.2.cloned.1.call-start = ((), (), s32[]{:S(2)}) async-start(), calls=%async_computation.5 | async-start | bytes 18874368 | tf_op jit(solution)/shard_map/reduce_scatter | solution.py:55
  82.9 1.2 copy-start.2
  148.5 17.9 %copy-start.8 = (s32[1,64]{1,0:T(1,128)S(1)}, s32[1,64]{1,0:T(1,128)}, u32[]{:S(2)}) copy-start(s32[1,64]{1,0:T(1,128)} %param.11) | copy-start | bytes 772
  154.4 143.6 %all-to-all-start = ((bf16[8,2,114688]{2,1,0:T(2,128)(2,1)}), bf16[8,2,114688]{2,1,0:T(2,128)(2,1)}, u32[]{:S(2)}, u32[]{:S(2)}) async-start(bf16[8,2,114688]{2,1,0:T(2,128)(2,1)} %reshape.260), calls=%async_computation.1 | async-start | bytes 7340032 | tf_op jit(solution)/shard_map/all_to_all | solution.py:37
  198.3 3.7 copy-start.3
  414.9 19.9 %copy-start.5 = (f32[64,8,16]{2,1,0:T(8,128)}, f32[64,8,16]{2,1,0:T(8,128)S(1)}, u32[]{:S(2)}) copy-start(f32[64,8,16]{2,1,0:T(8,128)S(1)} %get-tuple-element.29) | copy-start | bytes 98308
  427.3 124.6 %all-to-all-start.3 = ((f32[64,16,1024]{2,1,0:T(8,128)}), f32[64,16,1024]{2,1,0:T(8,128)}, u32[]{:S(2)}, u32[]{:S(2)}) async-start(f32[64,16,1024]{2,1,0:T(8,128)} %broadcast_select_fusion.3), calls=%async_computation.4 | async-start | bytes 8388608 | tf_op jit(solution)/shard_map/all_to_all | solution.py:90
  551.9 195.8 %all-to-all-start.2 = ((f32[64,16,1792]{2,1,0:T(8,128)}), f32[64,16,1792]{2,1,0:T(8,128)}, u32[]{:S(2)}, u32[]{:S(2)}) async-start(f32[64,16,1792]{2,1,0:T(8,128)} %broadcast_select_fusion), calls=%async_computation.3 | async-start | bytes 14680064 | tf_op jit(solution)/shard_map/all_to_all | solution.py:89
  577.3 23.2 %copy-start.1 = (bf16[64,16,1792]{2,1,0:T(8,128)(2,1)S(1)}, bf16[64,16,1792]{2,1,0:T(8,128)(2,1)}, u32[]{:S(2)}) copy-start(bf16[64,16,1792]{2,1,0:T(8,128)(2,1)} %gather_fusion.1) | copy-start | bytes 11010052
  759.7 16.2 %copy-start.7 = (f32[512]{0:T(512)S(1)}, f32[512]{0:T(512)}, u32[]{:S(2)}) copy-start(f32[512]{0:T(512)} %copy-done.6) | copy-start | bytes 6148
Sparse Core Ops, SparseCore 0:
  10.8 175.2 all-gather.1
  189.9 455.9 reduce-scatter.1
where the time goes:
time: 797 us; the launch traced here: 787 us
  waiting for transfers between devices  342 us (43%)
  local copies, waits for them, and re-layouts  220 us (28%)
  matrix products  75.1 us (9%)
  blocking collectives  69.7 us (9%)
  starting transfers between devices  38.3 us (5%)
  other arithmetic  27.5 us (3%)
  between operations  14.5 us (2%)
    all_to_all x1, waiting for transfers between devices, body(): lax.all_to_all(down_slots, 'tensor', split_axis=0, concat_axis=2, tiled=T...  143 us
    all_to_all x1, waiting for transfers between devices, body(): lax.all_to_all(up_slots, 'tensor', split_axis=0, concat_axis=2, tiled=True)  99.3 us
    unnamed x25, local copies, waits for them, and re-layouts  97 us
    all_to_all x1, waiting for transfers between devices, body(): lax.all_to_all(down_send, 'tensor', split_axis=2, concat_axis=0, tiled=True)  93.4 us
    psum x1, blocking collectives, body(): low_sum, back_sum = lax.psum((low_part, back_part), 'tensor')  58 us
    all_to_all x1, local copies, waits for them, and re-layouts, body(): lax.all_to_all(down_send, 'tensor', split_axis=2, concat_axis=0, tiled=True)  26.9 us
    dot_general x1, matrix products, body(): lax.dot_general(weight_cols, activations, (((0,), (1,)), ((), ())), prefe...  24.3 us
    select_n x1, local copies, waits for them, and re-layouts, body(): down_send = jnp.take(adapter_down, local_ids, axis=0)  24 us
  transfers between devices with their start and end apart: 6, of which 4 were waited for; matrix products, arithmetic and copies ran while one was open for 40% of the time, Pallas kernels for 0%

commit v1 on v0

v1 whole, which is shorter than its diff:
```python
import functools

import jax
import jax.numpy as jnp
from jax import lax
from jax.experimental import pallas as pl
from jax.experimental.pallas import tpu as pltpu
from jax.sharding import PartitionSpec as P

lowrank_scale = 0.5
live_total = 320

F32 = jnp.float32
BF16 = jnp.bfloat16


def dot(a, b, ca, cb):
    return lax.dot_general(a, b, (((ca,), (cb,)), ((), ())), preferred_element_type=F32)


def forward_kernel(x_ref, w_ref, out_ref):
    out_ref[0] = dot(x_ref[...], w_ref[...], 1, 0).astype(BF16)


def backward_kernel(g_ref, w_ref, rank_ref, down_ref, place_ref, out_ref, acc_ref):
    step = pl.program_id(0)

    @pl.when(step == 0)
    def _():
        acc_ref[...] = dot(rank_ref[...], down_ref[...], 1, 0)

    acc_ref[...] += dot(g_ref[0], w_ref[...], 1, 1)

    @pl.when(step == pl.num_programs(0) - 1)
    def _():
        rows = acc_ref[...].astype(BF16)
        out_ref[...] = dot(place_ref[...], rows, 0, 0).astype(BF16)


def body(activations, base_weight, adapter_down, adapter_up, block_adapter, block_live, cotangent):
    tensor_count = lax.axis_size("tensor")
    row_count, ff_dev = activations.shape
    d_dev = cotangent.shape[1]
    own_count, rank, _ = adapter_down.shape
    own_rows = own_count * rank
    wide = own_rows * tensor_count
    ids = block_adapter.reshape(-1)
    block_count = ids.shape[0]
    block_rows = row_count // block_count
    counts = block_live.reshape(-1)

    block_iota = jnp.arange(block_count, dtype=jnp.int32)
    first = jnp.sum(
        jnp.where(block_iota[None, :] < block_iota[:, None], counts[None, :], 0), axis=1
    )
    row_iota = jnp.arange(block_rows, dtype=jnp.int32)
    target = jnp.where(
        row_iota[None, :] < counts[:, None], first[:, None] + row_iota[None, :], -1
    ).reshape(1, row_count)
    live_iota = jnp.arange(live_total, dtype=jnp.int32)[:, None]
    place = (live_iota == target).astype(BF16)
    in_block = (live_iota >= first[None, :]) & (live_iota < (first + counts)[None, :])
    row_adapter = jnp.sum(jnp.where(in_block, ids[None, :], 0), axis=1, keepdims=True)
    wide_iota = jnp.arange(wide, dtype=jnp.int32)
    picked = row_adapter == (wide_iota // rank)[None, :]
    fold = ((wide_iota % rank)[:, None] == jnp.arange(rank, dtype=jnp.int32)[None, :]).astype(F32)

    grads = dot(place, cotangent, 1, 0).astype(BF16)
    grads_all = lax.all_gather(grads, "tensor", axis=0, tiled=False)
    acts = dot(place, activations, 1, 0).astype(BF16)

    send = jnp.concatenate(
        [
            adapter_down.reshape(own_rows, tensor_count, ff_dev),
            adapter_up.reshape(own_rows, tensor_count, d_dev),
        ],
        axis=2,
    ).transpose(1, 0, 2)
    adapters = lax.all_to_all(send, "tensor", split_axis=0, concat_axis=0, tiled=True)
    adapters = adapters.reshape(wide, ff_dev + d_dev)
    down_all, up_all = adapters[:, :ff_dev], adapters[:, ff_dev:]

    low_wide = jnp.where(picked, dot(acts, down_all, 1, 1), 0.0)
    back_wide = jnp.where(picked, dot(grads, up_all, 1, 1), 0.0)
    both = jnp.concatenate([low_wide, back_wide], axis=0)
    both = lax.dot_general(
        both, fold, (((1,), (0,)), ((), ())), precision=lax.Precision.HIGHEST,
        preferred_element_type=F32,
    )
    both = lax.psum(both, "tensor")
    low = both[:live_total].astype(BF16)
    back = (lowrank_scale * both[live_total:]).astype(BF16)
    fold_bf = fold.astype(BF16)
    low_spread = jnp.where(picked, dot(low, fold_bf, 1, 1), 0.0).astype(BF16)
    back_spread = jnp.where(picked, dot(back, fold_bf, 1, 1), 0.0).astype(BF16)

    params = pltpu.CompilerParams(vmem_limit_bytes=48 * 1024 * 1024)
    partial = pl.pallas_call(
        forward_kernel,
        grid=(tensor_count,),
        in_specs=[
            pl.BlockSpec((live_total, ff_dev), lambda j: (0, 0)),
            pl.BlockSpec((ff_dev, d_dev), lambda j: (0, j)),
        ],
        out_specs=pl.BlockSpec((1, live_total, d_dev), lambda j: (j, 0, 0)),
        out_shape=jax.ShapeDtypeStruct((tensor_count, live_total, d_dev), BF16),
        compiler_params=params,
    )(acts, base_weight)
    parts = lax.all_to_all(partial, "tensor", split_axis=0, concat_axis=0, tiled=True)

    grad_input = pl.pallas_call(
        backward_kernel,
        grid=(tensor_count,),
        in_specs=[
            pl.BlockSpec((1, live_total, d_dev), lambda j: (j, 0, 0)),
            pl.BlockSpec((ff_dev, d_dev), lambda j: (0, j)),
            pl.BlockSpec((live_total, wide), lambda j: (0, 0)),
            pl.BlockSpec((wide, ff_dev), lambda j: (0, 0)),
            pl.BlockSpec((live_total, row_count), lambda j: (0, 0)),
        ],
        out_specs=pl.BlockSpec((row_count, ff_dev), lambda j: (0, 0)),
        out_shape=jax.ShapeDtypeStruct((row_count, ff_dev), BF16),
        scratch_shapes=[pltpu.VMEM((live_total, ff_dev), F32)],
        compiler_params=params,
    )(grads_all, base_weight, back_spread, down_all, place)

    own_grads = jnp.concatenate(
        [dot(back_spread, acts, 0, 0), lowrank_scale * dot(low_spread, grads, 0, 0)], axis=1
    )
    own_grads = lax.psum(own_grads, "dp").astype(BF16)
    home = lax.all_to_all(
        own_grads.reshape(tensor_count, own_rows, ff_dev + d_dev),
        "tensor", split_axis=0, concat_axis=0, tiled=True,
    )
    down_own = home[:, :, :ff_dev].transpose(1, 0, 2).reshape(adapter_down.shape)
    up_own = home[:, :, ff_dev:].transpose(1, 0, 2).reshape(adapter_up.shape)

    base = jnp.sum(parts.astype(F32), axis=0)
    layer = (base + lowrank_scale * dot(low_spread, up_all, 1, 0)).astype(BF16)
    layer_out = dot(place, layer, 0, 0).astype(BF16)
    return layer_out, grad_input, down_own, up_own


def solution(mesh):
    in_specs = (
        P(("groups", "dp"), "tensor"),
        P("tensor", None),
        P(("groups", "tensor"), None, None),
        P(("groups", "tensor"), None, None),
        P(("groups", "dp"), None),
        P(("groups", "dp"), None),
        P(("groups", "dp"), "tensor"),
    )
    out_specs = (
        P(("groups", "dp"), "tensor"),
        P(("groups", "dp"), "tensor"),
        P(("groups", "tensor"), None, None),
        P(("groups", "tensor"), None, None),
    )
    return jax.shard_map(body, mesh=mesh, in_specs=in_specs, out_specs=out_specs, check_vma=False)
```

time: 797 us -> 363 us (0.46)
  local copies, waits for them, and re-layouts: 220 us -> 8.68 us
  waiting for transfers between devices: 342 us -> 216 us
  matrix products: 75.1 us -> 10.5 us
  Pallas kernels: 0 us -> 36.6 us
  blocking collectives: 69.7 us -> 46.3 us
  other arithmetic: 27.5 us -> 7.13 us
  starting transfers between devices: 38.3 us -> 19.1 us
    all_to_all x4 -> x3, waiting for transfers between devices: 342 us -> 215 us  [the longest x1 169 us: body(): lax.all_to_all(partial, 'tensor', split_axis=0, concat_axis=0, tiled=True)]
    unnamed x25 -> x16, local copies, waits for them, and re-layouts: 97 us -> 1.67 us
    dot_general x10, matrix products: 75.1 us -> 10.5 us  [the longest x9 10.1 us: dot(): lax.dot_general(a, b, (((ca,), (cb,)), ((), ())), preferred_element_type=...]
    all_to_all x4 -> x0, local copies, waits for them, and re-layouts: 55.8 us -> none  [the longest x1 26.9 us: body(): lax.all_to_all(down_send, 'tensor', split_axis=2, concat_axis=0, tiled=True)]
    select_n x2 -> x1, local copies, waits for them, and re-layouts: 38.6 us -> 0.09 us  [body(): jnp.where(row_iota[None, :] < counts[:, None], first[:, None] + row_iota[...]
    pallas_call x0 -> x2, Pallas kernels: none -> 36.6 us  [the longest x1 19.5 us: body(): pl.pallas_call(backward_kernel, grid=(tensor_count,), in_specs=[pl.BlockS...]
    gather x6 -> x0, local copies, waits for them, and re-layouts: 25.2 us -> none  [the longest x1 7.11 us: body(): down_slots = jnp.take(down_terms, block_of_slot, axis=0)]
    psum x2, blocking collectives: 69.7 us -> 46.3 us  [the longest x1 34.5 us: body(): both = lax.psum(both, 'tensor')]
  transfers between devices with their start and end apart: 6 -> 4, of which waited for: 4 -> 3; matrix products, arithmetic and copies ran while one was open for 40% -> 4% of each run, Pallas kernels for 0% -> 5%
where the time goes in v1:
time: 363 us; the launch traced here: 358 us
  waiting for transfers between devices  216 us (60%)
  blocking collectives  46.3 us (13%)
  Pallas kernels  36.6 us (10%)
  starting transfers between devices  19.1 us (5%)
  between operations  14.2 us (4%)
  matrix products  10.5 us (3%)
  local copies, waits for them, and re-layouts  8.68 us (2%)
  other arithmetic  7.13 us (2%)
    all_to_all x1, waiting for transfers between devices, body(): lax.all_to_all(partial, 'tensor', split_axis=0, concat_axis=0, tiled=True)  169 us
    psum x1, blocking collectives, body(): both = lax.psum(both, 'tensor')  34.5 us
    all_to_all x1, waiting for transfers between devices, body(): lax.all_to_all(send, 'tensor', split_axis=0, concat_axis=0, tiled=True)  29.7 us
    pallas_call x1, Pallas kernels, body(): pl.pallas_call(backward_kernel, grid=(tensor_count,), in_specs=[pl.BlockS...  19.5 us
    pallas_call x1, Pallas kernels, body(): pl.pallas_call(forward_kernel, grid=(tensor_count,), in_specs=[pl.BlockSp...  17.1 us
    all_to_all x1, waiting for transfers between devices, body(): lax.all_to_all(own_grads.reshape(tensor_count, own_rows, ff_dev + d_dev),...  16.4 us
    psum x1, blocking collectives, body(): own_grads = lax.psum(own_grads, 'dp').astype(BF16)  11.8 us
    dot_general x9, matrix products, dot(): lax.dot_general(a, b, (((ca,), (cb,)), ((), ())), preferred_element_type=...  10.1 us
  transfers between devices with their start and end apart: 4, of which 3 were waited for; matrix products, arithmetic and copies ran while one was open for 4% of the time, Pallas kernels for 5%

profile of v1, /device:TPU:28, one launch (start us, length us, event | category | flops | bytes accessed | tf_op | source)
XLA Modules:
  0.0 358.4 jit_solution(18169440535494059110)
XLA Ops:
  7.2 1.5 copy.24
  8.7 0.3 copy.20
  9.0 0.2 copy.23
  9.3 1.2 maximum_bitcast_fusion
  10.5 6.2 %all-to-all-start.1 = ((bf16[8,32,2816]{2,1,0:T(8,128)(2,1)}), bf16[8,32,2816]{2,1,0:T(8,128)(2,1)}, u32[]{:S(2)}, u32[]{:S(2)}) async-start(bf16[8,32,2816]{2,1,0:T(8,128)(2,1)} %maximum_bitcast_fusion), calls=%async_computation.1 | async-start | bytes 2883584 | tf_op jit(solution)/shard_map/all_to_all | solution.py:79
  17.1 1.4 convolution_convert_fusion.2
  18.5 0.8 convolution_convert_fusion.x_ref
  19.3 29.7 %all-to-all-done.1 = bf16[8,32,2816]{2,1,0:T(8,128)(2,1)} async-done(((bf16[8,32,2816]{2,1,0:T(8,128)(2,1)}), bf16[8,32,2816]{2,1,0:T(8,128)(2,1)}, u32[]{:S(2)}, u32[]{:S(2)}) %all-to-all-start.1) | async-done | bytes 1441824 | tf_op jit(solution)/shard_map/all_to_all | solution.py:79
  48.9 1.6 convolution_select_fusion.2
  50.6 1.7 convolution_select_fusion.3
  52.3 0.4 fusion.4
  52.7 34.5 %psum.14 = f32[640,16]{0,1:T(8,128)S(1)} all-reduce(f32[640,16]{0,1:T(8,128)S(1)} %fusion.4), channel_id=1, replica_groups=mesh['groups'=2,'dp'=2,'tensor'=8] {'tensor'}, use_global_device_ids=true, to_apply=%region_3.4 | all-reduce | flops 10240 | bytes 81920 | tf_op jit(solution)/shard_map/psum | solution.py:90
  87.2 0.3 fusion.2
  87.4 0.3 fusion.3.rank_ref
  87.8 0.5 convolution_multiply_fusion.1
  88.2 0.7 fusion.30
  88.9 1.8 pad_maximum_fusion
  90.7 11.8 %all-reduce.1 = bf16[256,2816]{1,0:T(8,128)(2,1)} all-reduce(f32[256,2816]{1,0:T(8,128)} %pad_maximum_fusion), channel_id=1, replica_groups=mesh['groups'=2,'dp'=2,'tensor'=8] {'dp'}, use_global_device_ids=true, to_apply=%region_4.5 | all-reduce | flops 720896 | bytes 4325376 | tf_op jit(solution)/shard_map/psum | solution.py:130
  102.5 6.8 %all-to-all-start.2 = ((bf16[8,32,2816]{2,1,0:T(8,128)(2,1)}), bf16[8,32,2816]{2,1,0:T(8,128)(2,1)S(1)}, u32[]{:S(2)}, u32[]{:S(2)}) async-start(bf16[8,32,2816]{2,1,0:T(8,128)(2,1)} %bitcast.32), calls=%async_computation.2 | async-start | bytes 2883584 | tf_op jit(solution)/shard_map/all_to_all | solution.py:131
  109.3 17.1 %shard_map.102 = bf16[8,320,1024]{2,1,0:T(8,128)(2,1)} custom-call(bf16[320,1792]{1,0:T(8,128)(2,1)S(1)} %convolution_convert_fusion.x_ref, bf16[1792,8192]{1,0:T(8,128)(2,1)} %w_ref.3), custom_call_target="tpu_custom_call" | custom-call | tf_op jit(solution)/shard_map/pallas_call | solution.py:98
  126.4 16.4 %all-to-all-done.2 = bf16[8,32,2816]{2,1,0:T(8,128)(2,1)S(1)} async-done(((bf16[8,32,2816]{2,1,0:T(8,128)(2,1)}), bf16[8,32,2816]{2,1,0:T(8,128)(2,1)S(1)}, u32[]{:S(2)}, u32[]{:S(2)}) %all-to-all-start.2) | async-done | bytes 1441824 | tf_op jit(solution)/shard_map/all_to_all | solution.py:131
  142.7 6.1 %all-to-all-start = ((bf16[8,320,1024]{2,1,0:T(8,128)(2,1)}), bf16[8,320,1024]{2,1,0:T(8,128)(2,1)}, u32[]{:S(2)}, u32[]{:S(2)}) async-start(bf16[8,320,1024]{2,1,0:T(8,128)(2,1)} %shard_map.102), calls=%async_computation | async-start | bytes 10485760 | tf_op jit(solution)/shard_map/all_to_all | solution.py:109
  148.9 0.7 all-gather.3.cloned.1.call-update
  149.7 1.2 slice.25.down_ref
  151.0 1.4 copy.21
  152.4 2.4 reshape.90
  154.8 0.3 copy.22
  155.1 1.0 reshape.91
  156.2 169.2 %all-to-all-done = bf16[8,320,1024]{2,1,0:T(8,128)(2,1)} async-done(((bf16[8,320,1024]{2,1,0:T(8,128)(2,1)}), bf16[8,320,1024]{2,1,0:T(8,128)(2,1)}, u32[]{:S(2)}, u32[]{:S(2)}) %all-to-all-start) | async-done | bytes 5242912 | tf_op jit(solution)/shard_map/all_to_all | solution.py:109
  325.4 3.8 %convert_reduce_fusion = f32[320,1024]{1,0:T(8,128)S(1)} fusion(bf16[8,320,1024]{2,1,0:T(8,128)(2,1)} %all-to-all-done), kind=kLoop, calls=%fused_computation | loop fusion | flops 4915200 | bytes 6553600 | tf_op jit(solution)/shard_map/reduce_sum | solution.py:138
  329.1 2.9 convolution_convert_fusion.1
  332.1 19.5 %shard_map.103 = bf16[512,1792]{1,0:T(8,128)(2,1)} custom-call(bf16[8,320,1024]{2,1,0:T(8,128)(2,1)} %bitcast.33, bf16[1792,8192]{1,0:T(8,128)(2,1)} %w_ref.3, bf16[320,256]{1,0:T(8,128)(2,1)S(1)} %fusion.3.rank_ref, bf16[256,1792]{1,0:T(8,128)(2,1)S(1)} %slice.25.down_ref, bf16[320,512]{1,0:T(8,128)(2,1)S(1)} %fusion.9.place_ref), custom_call_target="tpu_custom_call" | custom-call | tf_op jit(solution)/shard_map/pallas_call | solution.py:111
  (26 shorter events, 0.8 us)
Async XLA Ops:
  7.2 11.3 %copy-start = (bf16[512,1792]{1,0:T(8,128)(2,1)S(1)}, bf16[512,1792]{1,0:T(8,128)(2,1)}, u32[]{:S(2)}) copy-start(bf16[512,1792]{1,0:T(8,128)(2,1)} %param.7) | copy-start | bytes 5505028
  7.2 1.8 copy-start.3
  10.5 6.2 %copy-start.4 = (s32[1,64]{1,0:T(1,128)S(1)}, s32[1,64]{1,0:T(1,128)}, u32[]{:S(2)}) copy-start(s32[1,64]{1,0:T(1,128)} %param.12) | copy-start | bytes 772
  10.5 6.5 %copy-start.5 = (s32[1,64]{1,0:T(1,128)S(1)}, s32[1,64]{1,0:T(1,128)}, u32[]{:S(2)}) copy-start(s32[1,64]{1,0:T(1,128)} %param.11) | copy-start | bytes 772
  10.5 6.6 %copy-start.6 = (bf16[512,1024]{1,0:T(8,128)(2,1)S(1)}, bf16[512,1024]{1,0:T(8,128)(2,1)}, u32[]{:S(2)}) copy-start(bf16[512,1024]{1,0:T(8,128)(2,1)} %param.13) | copy-start | bytes 3145732
  10.5 38.4 %all-to-all-start.1 = ((bf16[8,32,2816]{2,1,0:T(8,128)(2,1)}), bf16[8,32,2816]{2,1,0:T(8,128)(2,1)}, u32[]{:S(2)}, u32[]{:S(2)}) async-start(bf16[8,32,2816]{2,1,0:T(8,128)(2,1)} %maximum_bitcast_fusion), calls=%async_computation.1 | async-start | bytes 2883584 | tf_op jit(solution)/shard_map/all_to_all | solution.py:79
  52.2 35.5 %copy-start.2 = (bf16[320,1024]{1,0:T(8,128)(2,1)S(1)}, bf16[320,1024]{1,0:T(8,128)(2,1)}, u32[]{:S(2)}) copy-start(bf16[320,1024]{1,0:T(8,128)(2,1)} %convolution_convert_fusion.2) | copy-start | bytes 1966084
  102.5 40.2 %all-to-all-start.2 = ((bf16[8,32,2816]{2,1,0:T(8,128)(2,1)}), bf16[8,32,2816]{2,1,0:T(8,128)(2,1)S(1)}, u32[]{:S(2)}, u32[]{:S(2)}) async-start(bf16[8,32,2816]{2,1,0:T(8,128)(2,1)} %bitcast.32), calls=%async_computation.2 | async-start | bytes 2883584 | tf_op jit(solution)/shard_map/all_to_all | solution.py:131
  142.7 182.6 %all-to-all-start = ((bf16[8,320,1024]{2,1,0:T(8,128)(2,1)}), bf16[8,320,1024]{2,1,0:T(8,128)(2,1)}, u32[]{:S(2)}, u32[]{:S(2)}) async-start(bf16[8,320,1024]{2,1,0:T(8,128)(2,1)} %shard_map.102), calls=%async_computation | async-start | bytes 10485760 | tf_op jit(solution)/shard_map/all_to_all | solution.py:109
  148.9 183.2 %all-gather.3.cloned.1.call-start = ((), (), s32[]{:S(2)}) async-start(), calls=%async_computation.3 | async-start | bytes 5898240 | tf_op jit(solution)/shard_map/all_gather | solution.py:69
  332.1 19.5 %copy-start.1 = (bf16[512,1792]{1,0:T(8,128)(2,1)S(1)}, bf16[512,1792]{1,0:T(8,128)(2,1)}, u32[]{:S(2)}) copy-start(bf16[512,1792]{1,0:T(8,128)(2,1)} %param.7) | copy-start | bytes 5505028
Sparse Core Ops, SparseCore 0:
  151.9 167.0 all-gather.2

commit v2 on v1

--- a/solution.py
+++ b/solution.py
@@ -18,23 +18,179 @@
     return lax.dot_general(a, b, (((ca,), (cb,)), ((), ())), preferred_element_type=F32)
 
 
-def forward_kernel(x_ref, w_ref, out_ref):
-    out_ref[0] = dot(x_ref[...], w_ref[...], 1, 0).astype(BF16)
-
-
-def backward_kernel(g_ref, w_ref, rank_ref, down_ref, place_ref, out_ref, acc_ref):
-    step = pl.program_id(0)
-
-    @pl.when(step == 0)
-    def _():
-        acc_ref[...] = dot(rank_ref[...], down_ref[...], 1, 0)
-
-    acc_ref[...] += dot(g_ref[0], w_ref[...], 1, 1)
-
-    @pl.when(step == pl.num_programs(0) - 1)
-    def _():
-        rows = acc_ref[...].astype(BF16)
-        out_ref[...] = dot(place_ref[...], rows, 0, 0).astype(BF16)
+def base_kernel(
+    count, acts_ref, grads_ref, w_ref, base_ref, through_ref,
+    gathered, pair_out, pair_in, line_out, line_in, kept, tiles, tile_sem,
+    own_send, near_send, pass_send, gather_recv, pair_send, pair_recv, line_send, line_recv,
+):
+    d_dev = grads_ref.shape[1]
+    lines = count // 2
+    me = lax.axis_index("tensor")
+    p = lax.rem(me, 2)
+    q = lax.div(me, 2)
+    near = q * 2 + (1 - p)
+
+    def ahead(k):
+        return lax.rem(q + 1 + k, lines)
+
+    def behind(k):
+        return lax.rem(q - 1 - k + lines, lines)
+
+    def tile(chunk, step):
+        slot = lax.rem(step, 2)
+        columns = pl.ds(pl.multiple_of(chunk * d_dev, d_dev), d_dev)
+        return pltpu.make_async_copy(w_ref.at[:, columns], tiles.at[slot], tile_sem.at[slot])
+
+    def chunk_of(step):
+        k = lax.rem(step, lines)
+        back_side = jnp.where(step < 3 * lines, p, 1 - p)
+        line = jnp.where(step < 2 * lines, ahead(k), lax.rem(q - k + lines, lines))
+        side = jnp.where(step < lines, 1 - p, jnp.where(step < 2 * lines, p, back_side))
+        return line * 2 + side
+
+    def weights(step):
+        @pl.when(step + 1 < 4 * lines)
+        def _():
+            tile(chunk_of(step + 1), step + 1).start()
+
+        tile(chunk_of(step), step).wait()
+        return tiles[lax.rem(step, 2)]
+
+    def remote(src, dst, send, recv, target):
+        return pltpu.make_async_remote_copy(
+            src_ref=src, dst_ref=dst, send_sem=send, recv_sem=recv,
+            device_id={"tensor": target}, device_id_type=pl.DeviceIdType.MESH,
+        )
+
+    def own_copy(k):
+        target = ahead(k) * 2 + p
+        return remote(grads_ref, gathered.at[me], own_send.at[k], gather_recv.at[me], target)
+
+    def near_copy():
+        return remote(grads_ref, gathered.at[me], near_send, gather_recv.at[me], near)
+
+    def pass_copy(k):
+        chunk = behind(k) * 2 + p
+        return remote(
+            gathered.at[chunk], gathered.at[chunk], pass_send.at[k], gather_recv.at[chunk], near
+        )
+
+    def arrival(chunk):
+        return remote(grads_ref, gathered.at[chunk], near_send, gather_recv.at[chunk], near)
+
+    def pair_copy(k):
+        return remote(pair_out.at[k], pair_in.at[k], pair_send.at[k], pair_recv.at[k], near)
+
+    def line_copy(k):
+        target = ahead(k) * 2 + p
+        return remote(line_out.at[k], line_in.at[k], line_send.at[k], line_recv.at[k], target)
+
+    tile(chunk_of(0), 0).start()
+    barrier = pltpu.get_barrier_semaphore()
+
+    def greet(target):
+        pl.semaphore_signal(
+            barrier, inc=1, device_id={"tensor": target}, device_id_type=pl.DeviceIdType.MESH
+        )
+
+    greet(near)
+
+    @pl.loop(0, lines - 1)
+    def _(k):
+        greet(ahead(k) * 2 + p)
+
+    pl.semaphore_wait(barrier, lines)
+
+    @pl.loop(0, lines - 1)
+    def _(k):
+        own_copy(k).start()
+
+    @pl.loop(0, lines)
+    def _(k):
+        w = weights(k)
+        pair_out[k] = dot(acts_ref[...], w, 1, 0).astype(BF16)
+        pair_copy(k).start()
+
+    near_copy().start()
+    gathered[me] = grads_ref[...]
+
+    @pl.loop(0, lines)
+    def _(k):
+        w = weights(lines + k)
+        kept[...] = dot(acts_ref[...], w, 1, 0)
+        pair_copy(k).wait_recv()
+
+        @pl.when(k < lines - 1)
+        def _():
+            line_out[k] = (kept[...] + pair_in[k].astype(F32)).astype(BF16)
+            line_copy(k).start()
+            arrival(behind(k) * 2 + p).wait_recv()
+            pass_copy(k).start()
+
+    base_ref[...] = kept[...] + pair_in[lines - 1].astype(F32)
+    through_ref[...] = jnp.zeros_like(through_ref)
+
+    @pl.loop(0, 2 * lines)
+    def _(k):
+        chunk = chunk_of(2 * lines + k)
+
+        @pl.when(k >= lines)
+        def _():
+            arrival(chunk).wait_recv()
+
+        w = weights(2 * lines + k)
+        through_ref[...] += dot(gathered[chunk], w, 1, 1)
+
+    @pl.loop(0, lines - 1)
+    def _(k):
+        line_copy(k).wait_recv()
+        base_ref[...] += line_in[k].astype(F32)
+        line_copy(k).wait_send()
+        own_copy(k).wait_send()
+        pass_copy(k).wait_send()
+
+    near_copy().wait_send()
+
+    @pl.loop(0, lines)
+    def _(k):
+        pair_copy(k).wait_send()
+
+
+def base_products(count, acts, grads, base_weight):
+    rows, ff_dev = acts.shape
+    d_dev = grads.shape[1]
+    lines = count // 2
+    vmem = pl.BlockSpec(memory_space=pltpu.VMEM)
+    dma = pltpu.SemaphoreType.DMA
+    return pl.pallas_call(
+        functools.partial(base_kernel, count),
+        in_specs=[vmem, vmem, pl.BlockSpec(memory_space=pl.ANY)],
+        out_specs=[vmem, vmem],
+        out_shape=[
+            jax.ShapeDtypeStruct((rows, d_dev), F32),
+            jax.ShapeDtypeStruct((rows, ff_dev), F32),
+        ],
+        scratch_shapes=[
+            pltpu.VMEM((count, rows, d_dev), BF16),
+            pltpu.VMEM((lines, rows, d_dev), BF16),
+            pltpu.VMEM((lines, rows, d_dev), BF16),
+            pltpu.VMEM((lines, rows, d_dev), BF16),
+            pltpu.VMEM((lines, rows, d_dev), BF16),
+            pltpu.VMEM((rows, d_dev), F32),
+            pltpu.VMEM((2, ff_dev, d_dev), BF16),
+            dma((2,)),
+            dma((lines,)), dma, dma((lines,)), dma((count,)),
+            dma((lines,)), dma((lines,)), dma((lines,)), dma((lines,)),
+        ],
+        compiler_params=pltpu.CompilerParams(
+            collective_id=0, has_side_effects=True, vmem_limit_bytes=52 * 1024 * 1024
+        ),
+        cost_estimate=pl.CostEstimate(
+            flops=4 * rows * ff_dev * d_dev * count,
+            bytes_accessed=10 * ff_dev * d_dev * count,
+            transcendentals=0,
+        ),
+    )(acts, grads, base_weight)
 
 
 def body(activations, base_weight, adapter_down, adapter_up, block_adapter, block_live, cotangent):
@@ -66,7 +222,6 @@
     fold = ((wide_iota % rank)[:, None] == jnp.arange(rank, dtype=jnp.int32)[None, :]).astype(F32)
 
     grads = dot(place, cotangent, 1, 0).astype(BF16)
-    grads_all = lax.all_gather(grads, "tensor", axis=0, tiled=False)
     acts = dot(place, activations, 1, 0).astype(BF16)
 
     send = jnp.concatenate(
@@ -77,6 +232,7 @@
         axis=2,
     ).transpose(1, 0, 2)
     adapters = lax.all_to_all(send, "tensor", split_axis=0, concat_axis=0, tiled=True)
+    base, through = base_products(tensor_count, acts, grads, base_weight)
     adapters = adapters.reshape(wide, ff_dev + d_dev)
     down_all, up_all = adapters[:, :ff_dev], adapters[:, ff_dev:]
 
@@ -94,35 +250,8 @@
     low_spread = jnp.where(picked, dot(low, fold_bf, 1, 1), 0.0).astype(BF16)
     back_spread = jnp.where(picked, dot(back, fold_bf, 1, 1), 0.0).astype(BF16)
 
-    params = pltpu.CompilerParams(vmem_limit_bytes=48 * 1024 * 1024)
-    partial = pl.pallas_call(
-        forward_kernel,
-        grid=(tensor_count,),
-        in_specs=[
-            pl.BlockSpec((live_total, ff_dev), lambda j: (0, 0)),
-            pl.BlockSpec((ff_dev, d_dev), lambda j: (0, j)),
-        ],
-        out_specs=pl.BlockSpec((1, live_total, d_dev), lambda j: (j, 0, 0)),
-        out_shape=jax.ShapeDtypeStruct((tensor_count, live_total, d_dev), BF16),
-        compiler_params=params,
-    )(acts, base_weight)
-    parts = lax.all_to_all(partial, "tensor", split_axis=0, concat_axis=0, tiled=True)
-
-    grad_input = pl.pallas_call(
-        backward_kernel,
-        grid=(tensor_count,),
-        in_specs=[
-            pl.BlockSpec((1, live_total, d_dev), lambda j: (j, 0, 0)),
-            pl.BlockSpec((ff_dev, d_dev), lambda j: (0, j)),
-            pl.BlockSpec((live_total, wide), lambda j: (0, 0)),
-            pl.BlockSpec((wide, ff_dev), lambda j: (0, 0)),
-            pl.BlockSpec((live_total, row_count), lambda j: (0, 0)),
-        ],
-        out_specs=pl.BlockSpec((row_count, ff_dev), lambda j: (0, 0)),
-        out_shape=jax.ShapeDtypeStruct((row_count, ff_dev), BF16),
-        scratch_shapes=[pltpu.VMEM((live_total, ff_dev), F32)],
-        compiler_params=params,
-    )(grads_all, base_weight, back_spread, down_all, place)
+    through = through + dot(back_spread, down_all, 1, 0)
+    grad_input = dot(place, through.astype(BF16), 0, 0).astype(BF16)
 
     own_grads = jnp.concatenate(
         [dot(back_spread, acts, 0, 0), lowrank_scale * dot(low_spread, grads, 0, 0)], axis=1
@@ -135,7 +264,6 @@
     down_own = home[:, :, :ff_dev].transpose(1, 0, 2).reshape(adapter_down.shape)
     up_own = home[:, :, ff_dev:].transpose(1, 0, 2).reshape(adapter_up.shape)
 
-    base = jnp.sum(parts.astype(F32), axis=0)
     layer = (base + lowrank_scale * dot(low_spread, up_all, 1, 0)).astype(BF16)
     layer_out = dot(place, layer, 0, 0).astype(BF16)
     return layer_out, grad_input, down_own, up_own

time: 363 us -> 267 us (0.74); the launches traced: 358 us -> 266 us
  waiting for transfers between devices: 216 us -> 29.7 us
  Pallas kernels: 36.6 us -> 147 us
  between operations: 14.2 us -> 0.79 us
  matrix products: 10.5 us -> 16.6 us
  starting transfers between devices: 19.1 us -> 13.6 us
  other arithmetic: 7.13 us -> 2.23 us
    all_to_all x1 -> x0, waiting for transfers between devices: 169 us -> none  [body(): lax.all_to_all(partial, 'tensor', split_axis=0, concat_axis=0, tiled=True)]
    pallas_call x2 -> x1, Pallas kernels: 36.6 us -> 147 us  [base_products(): pl.pallas_call(functools.partial(base_kernel, count), in_specs=[vmem, vme...]
    all_to_all x1, waiting for transfers between devices: 16.4 us -> 0.01 us  [body(): lax.all_to_all(own_grads.reshape(tensor_count, own_rows, ff_dev + d_dev),...]
    dot_general x9 -> x10, matrix products: 10.1 us -> 16.2 us  [dot(): lax.dot_general(a, b, (((ca,), (cb,)), ((), ())), preferred_element_type=...]
    all_to_all x1 -> x0, starting transfers between devices: 6.13 us -> none  [body(): lax.all_to_all(partial, 'tensor', split_axis=0, concat_axis=0, tiled=True)]
    reduce_sum x1 -> x0, other arithmetic: 3.76 us -> none  [body(): base = jnp.sum(parts.astype(F32), axis=0)]
  transfers between devices with their start and end apart: 4 -> 2, of which waited for: 3 -> 1; matrix products, arithmetic and copies ran while one was open for 4% -> 4% of each run, Pallas kernels for 5% -> 55%
where the time goes in v2:
time: 267 us; the launch traced here: 266 us
  Pallas kernels  147 us (55%)
  blocking collectives  46.3 us (17%)
  waiting for transfers between devices  29.7 us (11%)
  matrix products  16.6 us (6%)
  starting transfers between devices  13.6 us (5%)
  local copies, waits for them, and re-layouts  9.67 us (4%)
    pallas_call x1, Pallas kernels, base_products(): pl.pallas_call(functools.partial(base_kernel, count), in_specs=[vmem, vme...  147 us
    psum x1, blocking collectives, body(): both = lax.psum(both, 'tensor')  34.5 us
    all_to_all x1, waiting for transfers between devices, body(): lax.all_to_all(send, 'tensor', split_axis=0, concat_axis=0, tiled=True)  29.7 us
    dot_general x10, matrix products, dot(): lax.dot_general(a, b, (((ca,), (cb,)), ((), ())), preferred_element_type=...  16.2 us
    psum x1, blocking collectives, body(): own_grads = lax.psum(own_grads, 'dp').astype(BF16)  11.8 us
    all_to_all x1, starting transfers between devices, body(): lax.all_to_all(own_grads.reshape(tensor_count, own_rows, ff_dev + d_dev),...  7.47 us
    all_to_all x1, starting transfers between devices, body(): lax.all_to_all(send, 'tensor', split_axis=0, concat_axis=0, tiled=True)  6.16 us
  transfers between devices with their start and end apart: 2, of which 1 were waited for; matrix products, arithmetic and copies ran while one was open for 4% of the time, Pallas kernels for 55%

profile of v2, /device:TPU:28, one launch (start us, length us, event | category | flops | bytes accessed | tf_op | source)
XLA Modules:
  0.0 266.1 jit_solution(3948082762012903421)
XLA Ops:
  0.7 1.5 copy.25
  2.2 0.2 copy.24
  2.3 0.1 maximum_bitcast_fusion
  2.4 1.3 copy.21
  3.8 6.2 %all-to-all-start = ((bf16[8,32,2816]{2,1,0:T(8,128)(2,1)}), bf16[8,32,2816]{2,1,0:T(8,128)(2,1)}, u32[]{:S(2)}, u32[]{:S(2)}) async-start(bf16[8,32,2816]{2,1,0:T(8,128)(2,1)} %copy.21), calls=%async_computation | async-start | bytes 2883584 | tf_op jit(solution)/shard_map/all_to_all | solution.py:234
  9.9 0.1 select_reduce_fusion.1
  10.0 0.1 add_select_fusion
  10.2 0.1 select_reduce_fusion
  10.4 1.4 convolution_convert_fusion.3.grads_ref
  11.7 0.8 convolution_convert_fusion.1.acts_ref
  12.5 29.7 %all-to-all-done = bf16[8,32,2816]{2,1,0:T(8,128)(2,1)} async-done(((bf16[8,32,2816]{2,1,0:T(8,128)(2,1)}), bf16[8,32,2816]{2,1,0:T(8,128)(2,1)}, u32[]{:S(2)}, u32[]{:S(2)}) %all-to-all-start) | async-done | bytes 1441824 | tf_op jit(solution)/shard_map/all_to_all | solution.py:234
  42.2 1.6 convolution_select_fusion.2
  43.8 1.7 convolution_select_fusion.3
  45.5 0.4 fusion.8
  45.9 34.5 %psum.14 = f32[640,16]{0,1:T(8,128)S(1)} all-reduce(f32[640,16]{0,1:T(8,128)S(1)} %fusion.8), channel_id=1, replica_groups=mesh['groups'=2,'dp'=2,'tensor'=8] {'tensor'}, use_global_device_ids=true, to_apply=%region_2.3 | all-reduce | flops 10240 | bytes 81920 | tf_op jit(solution)/shard_map/psum | solution.py:246
  80.4 0.3 fusion.3
  80.7 0.3 fusion.4
  81.0 1.5 convolution_multiply_fusion.1
  82.5 0.7 fusion.33
  83.2 1.8 pad_maximum_fusion
  85.0 11.8 %all-reduce.1 = bf16[256,2816]{1,0:T(8,128)(2,1)} all-reduce(f32[256,2816]{1,0:T(8,128)} %pad_maximum_fusion), channel_id=1, replica_groups=mesh['groups'=2,'dp'=2,'tensor'=8] {'dp'}, use_global_device_ids=true, to_apply=%region_3.4 | all-reduce | flops 720896 | bytes 4325376 | tf_op jit(solution)/shard_map/psum | solution.py:259
  96.8 7.5 %all-to-all-start.1 = ((bf16[8,32,2816]{2,1,0:T(8,128)(2,1)}), bf16[8,32,2816]{2,1,0:T(8,128)(2,1)}, u32[]{:S(2)}, u32[]{:S(2)}) async-start(bf16[8,32,2816]{2,1,0:T(8,128)(2,1)} %bitcast.32), calls=%async_computation.1 | async-start | bytes 2883584 | tf_op jit(solution)/shard_map/all_to_all | solution.py:260
  104.3 1.1 copy-done.1
  105.4 147.1 %shard_map.102 = (f32[320,1024]{1,0:T(8,128)}, f32[320,1792]{1,0:T(8,128)}) custom-call(bf16[320,1792]{1,0:T(8,128)(2,1)S(1)} %convolution_convert_fusion.1.acts_ref, bf16[320,1024]{1,0:T(8,128)(2,1)S(1)} %copy-done.1, bf16[1792,8192]{1,0:T(8,128)(2,1)} %w_ref.1), custom_call_target="tpu_custom_call" | custom-call | flops 18790481920 | bytes 146800640 | tf_op jit(solution)/shard_map/pallas_call | solution.py:165
  252.5 3.4 %convolution_convert_fusion.2 = bf16[512,1024]{1,0:T(8,128)(2,1)} fusion(f32[320,1024]{1,0:T(8,128)} %get-tuple-element.6, bf16[320,256]{1,0:T(8,128)(2,1)S(1)} %fusion.3, bf16[256,2816]{1,0:T(8,128)(2,1)} %bitcast.5, s32[512]{0:T(512)S(1)} %select_n.58), kind=kOutput, calls=%fused_computation.5 | convolution fusion | flops 504987648 | bytes 3049472 | tf_op jit(solution)/shard_map/dot_general | solution.py:18
  255.9 4.6 %convolution_convert_fusion = bf16[512,1792]{1,0:T(8,128)(2,1)} fusion(f32[320,1792]{1,0:T(8,128)} %get-tuple-element.7, bf16[320,256]{1,0:T(8,128)(2,1)S(1)} %fusion.4, bf16[256,2816]{1,0:T(8,128)(2,1)} %bitcast.5, s32[512]{0:T(512)S(1)} %select_n.58), kind=kOutput, calls=%fused_computation | convolution fusion | flops 883032064 | bytes 5212160 | tf_op jit(solution)/shard_map/dot_general | solution.py:18
  260.5 1.2 slice_bitcast_fusion
  261.8 0.5 copy.22
  262.3 1.3 reshape.90
  263.6 1.1 slice_bitcast_fusion.1
  264.7 0.3 copy.23
  265.0 1.0 reshape.91
  (15 shorter events, 0.1 us)
Async XLA Ops:
  0.6 11.1 %copy-start = (bf16[512,1792]{1,0:T(8,128)(2,1)S(1)}, bf16[512,1792]{1,0:T(8,128)(2,1)}, u32[]{:S(2)}) copy-start(bf16[512,1792]{1,0:T(8,128)(2,1)} %param.7) | copy-start | bytes 5505028
  0.6 1.5 copy-start.2
  3.8 6.2 %copy-start.3 = (s32[1,64]{1,0:T(1,128)S(1)}, s32[1,64]{1,0:T(1,128)}, u32[]{:S(2)}) copy-start(s32[1,64]{1,0:T(1,128)} %param.12) | copy-start | bytes 772
  3.8 6.5 %copy-start.4 = (s32[1,64]{1,0:T(1,128)S(1)}, s32[1,64]{1,0:T(1,128)}, u32[]{:S(2)}) copy-start(s32[1,64]{1,0:T(1,128)} %param.11) | copy-start | bytes 772
  3.8 6.6 %copy-start.5 = (bf16[512,1024]{1,0:T(8,128)(2,1)S(1)}, bf16[512,1024]{1,0:T(8,128)(2,1)}, u32[]{:S(2)}) copy-start(bf16[512,1024]{1,0:T(8,128)(2,1)} %param.13) | copy-start | bytes 3145732
  3.8 38.4 %all-to-all-start = ((bf16[8,32,2816]{2,1,0:T(8,128)(2,1)}), bf16[8,32,2816]{2,1,0:T(8,128)(2,1)}, u32[]{:S(2)}, u32[]{:S(2)}) async-start(bf16[8,32,2816]{2,1,0:T(8,128)(2,1)} %copy.21), calls=%async_computation | async-start | bytes 2883584 | tf_op jit(solution)/shard_map/all_to_all | solution.py:234
  96.8 163.7 %all-to-all-start.1 = ((bf16[8,32,2816]{2,1,0:T(8,128)(2,1)}), bf16[8,32,2816]{2,1,0:T(8,128)(2,1)}, u32[]{:S(2)}, u32[]{:S(2)}) async-start(bf16[8,32,2816]{2,1,0:T(8,128)(2,1)} %bitcast.32), calls=%async_computation.1 | async-start | bytes 2883584 | tf_op jit(solution)/shard_map/all_to_all | solution.py:260
  104.3 1.1 copy-start.1

commit v3 on v2

--- a/solution.py
+++ b/solution.py
@@ -21,7 +21,7 @@
 def base_kernel(
     count, acts_ref, grads_ref, w_ref, base_ref, through_ref,
     gathered, pair_out, pair_in, line_out, line_in, kept, tiles, tile_sem,
-    own_send, near_send, pass_send, gather_recv, pair_send, pair_recv, line_send, line_recv,
+    up_send, down_send, near_send, pass_send, gather_recv, pair_send, pair_recv, line_send, line_recv,
 ):
     d_dev = grads_ref.shape[1]
     lines = count // 2
@@ -29,12 +29,10 @@
     p = lax.rem(me, 2)
     q = lax.div(me, 2)
     near = q * 2 + (1 - p)
+    turn = jnp.where(q * 2 < lines, 1, -1)
 
     def ahead(k):
         return lax.rem(q + 1 + k, lines)
-
-    def behind(k):
-        return lax.rem(q - 1 - k + lines, lines)
 
     def tile(chunk, step):
         slot = lax.rem(step, 2)
@@ -44,7 +42,7 @@
     def chunk_of(step):
         k = lax.rem(step, lines)
         back_side = jnp.where(step < 3 * lines, p, 1 - p)
-        line = jnp.where(step < 2 * lines, ahead(k), lax.rem(q - k + lines, lines))
+        line = jnp.where(step < 2 * lines, ahead(k), lax.rem(q + turn * k + lines, lines))
         side = jnp.where(step < lines, 1 - p, jnp.where(step < 2 * lines, p, back_side))
         return line * 2 + side
 
@@ -62,18 +60,28 @@
             device_id={"tensor": target}, device_id_type=pl.DeviceIdType.MESH,
         )
 
-    def own_copy(k):
-        target = ahead(k) * 2 + p
-        return remote(grads_ref, gathered.at[me], own_send.at[k], gather_recv.at[me], target)
-
     def near_copy():
         return remote(grads_ref, gathered.at[me], near_send, gather_recv.at[me], near)
 
-    def pass_copy(k):
-        chunk = behind(k) * 2 + p
+    def pass_copy(line):
+        chunk = line * 2 + p
         return remote(
-            gathered.at[chunk], gathered.at[chunk], pass_send.at[k], gather_recv.at[chunk], near
-        )
+            gathered.at[chunk], gathered.at[chunk], pass_send.at[line], gather_recv.at[chunk], near
+        )
+
+    def first_hop(sends, line):
+        target = line * 2 + p
+        return remote(grads_ref, gathered.at[me], sends.at[0], gather_recv.at[me], target)
+
+    def hop(distance, source, sends, line):
+        chunk = source * 2 + p
+        return remote(
+            gathered.at[chunk], gathered.at[chunk], sends.at[distance],
+            gather_recv.at[chunk], line * 2 + p,
+        )
+
+    has_up = q + 1 < lines
+    has_down = q > 0
 
     def arrival(chunk):
         return remote(grads_ref, gathered.at[chunk], near_send, gather_recv.at[chunk], near)
@@ -101,9 +109,13 @@
 
     pl.semaphore_wait(barrier, lines)
 
-    @pl.loop(0, lines - 1)
-    def _(k):
-        own_copy(k).start()
+    @pl.when(has_up)
+    def _():
+        first_hop(up_send, q + 1).start()
+
+    @pl.when(has_down)
+    def _():
+        first_hop(down_send, q - 1).start()
 
     @pl.loop(0, lines)
     def _(k):
@@ -124,8 +136,27 @@
         def _():
             line_out[k] = (kept[...] + pair_in[k].astype(F32)).astype(BF16)
             line_copy(k).start()
-            arrival(behind(k) * 2 + p).wait_recv()
-            pass_copy(k).start()
+            below, above = q - 1 - k, q + 1 + k
+
+            @pl.when(below >= 0)
+            def _():
+                arrival(below * 2 + p).wait_recv()
+
+                @pl.when(has_up)
+                def _():
+                    hop(k + 1, below, up_send, q + 1).start()
+
+                pass_copy(below).start()
+
+            @pl.when(above < lines)
+            def _():
+                arrival(above * 2 + p).wait_recv()
+
+                @pl.when(has_down)
+                def _():
+                    hop(k + 1, above, down_send, q - 1).start()
+
+                pass_copy(above).start()
 
     base_ref[...] = kept[...] + pair_in[lines - 1].astype(F32)
     through_ref[...] = jnp.zeros_like(through_ref)
@@ -146,14 +177,114 @@
         line_copy(k).wait_recv()
         base_ref[...] += line_in[k].astype(F32)
         line_copy(k).wait_send()
-        own_copy(k).wait_send()
-        pass_copy(k).wait_send()
+        below, above = q - 1 - k, q + 1 + k
+
+        @pl.when(below >= 0)
+        def _():
+            pass_copy(below).wait_send()
+
+            @pl.when(has_up)
+            def _():
+                hop(k + 1, below, up_send, q + 1).wait_send()
+
+        @pl.when(above < lines)
+        def _():
+            pass_copy(above).wait_send()
+
+            @pl.when(has_down)
+            def _():
+                hop(k + 1, above, down_send, q - 1).wait_send()
+
+    @pl.when(has_up)
+    def _():
+        first_hop(up_send, q + 1).wait_send()
+
+    @pl.when(has_down)
+    def _():
+        first_hop(down_send, q - 1).wait_send()
 
     near_copy().wait_send()
 
     @pl.loop(0, lines)
     def _(k):
         pair_copy(k).wait_send()
+
+
+def rank_kernel(count, part_ref, out_ref, pair_in, line_in, pair_send, pair_recv, line_send, line_recv):
+    lines = count // 2
+    me = lax.axis_index("tensor")
+    p = lax.rem(me, 2)
+    q = lax.div(me, 2)
+    near = q * 2 + (1 - p)
+    barrier = pltpu.get_barrier_semaphore()
+
+    def ahead(k):
+        return lax.rem(q + 1 + k, lines)
+
+    def greet(target):
+        pl.semaphore_signal(
+            barrier, inc=1, device_id={"tensor": target}, device_id_type=pl.DeviceIdType.MESH
+        )
+
+    def line_copy(source, k, target):
+        return pltpu.make_async_remote_copy(
+            src_ref=line_in.at[source], dst_ref=line_in.at[source],
+            send_sem=line_send.at[k], recv_sem=line_recv.at[source],
+            device_id={"tensor": target * 2 + p}, device_id_type=pl.DeviceIdType.MESH,
+        )
+
+    greet(near)
+
+    @pl.loop(0, lines - 1)
+    def _(k):
+        greet(ahead(k) * 2 + p)
+
+    pl.semaphore_wait(barrier, lines)
+    pair = pltpu.make_async_remote_copy(
+        src_ref=part_ref, dst_ref=pair_in, send_sem=pair_send, recv_sem=pair_recv,
+        device_id={"tensor": near}, device_id_type=pl.DeviceIdType.MESH,
+    )
+    pair.start()
+    pair.wait()
+    line_in[q] = part_ref[...] + pair_in[...]
+
+    @pl.loop(0, lines - 1)
+    def _(k):
+        line_copy(q, k, ahead(k)).start()
+
+    @pl.loop(0, lines - 1)
+    def _(k):
+        line_copy(ahead(k), k, ahead(k)).wait_recv()
+
+    out_ref[...] = line_in[0]
+
+    @pl.loop(1, lines)
+    def _(k):
+        out_ref[...] += line_in[k]
+
+    @pl.loop(0, lines - 1)
+    def _(k):
+        line_copy(q, k, ahead(k)).wait_send()
+
+
+def rank_sums(count, part):
+    lines = count // 2
+    vmem = pl.BlockSpec(memory_space=pltpu.VMEM)
+    dma = pltpu.SemaphoreType.DMA
+    return pl.pallas_call(
+        functools.partial(rank_kernel, count),
+        in_specs=[vmem],
+        out_specs=vmem,
+        out_shape=jax.ShapeDtypeStruct(part.shape, F32),
+        scratch_shapes=[
+            pltpu.VMEM(part.shape, F32),
+            pltpu.VMEM((lines,) + part.shape, F32),
+            dma, dma, dma((lines,)), dma((lines,)),
+        ],
+        compiler_params=pltpu.CompilerParams(
+            collective_id=1, has_side_effects=True, vmem_limit_bytes=16 * 1024 * 1024
+        ),
+    )(part)
 
 
 def base_products(count, acts, grads, base_weight):
@@ -179,7 +310,7 @@
             pltpu.VMEM((rows, d_dev), F32),
             pltpu.VMEM((2, ff_dev, d_dev), BF16),
             dma((2,)),
-            dma((lines,)), dma, dma((lines,)), dma((count,)),
+            dma((lines,)), dma((lines,)), dma, dma((lines,)), dma((count,)),
             dma((lines,)), dma((lines,)), dma((lines,)), dma((lines,)),
         ],
         compiler_params=pltpu.CompilerParams(
@@ -240,15 +371,15 @@
     back_wide = jnp.where(picked, dot(grads, up_all, 1, 1), 0.0)
     both = jnp.concatenate([low_wide, back_wide], axis=0)
     both = lax.dot_general(
-        both, fold, (((1,), (0,)), ((), ())), precision=lax.Precision.HIGHEST,
+        fold, both, (((0,), (1,)), ((), ())), precision=lax.Precision.HIGHEST,
         preferred_element_type=F32,
     )
-    both = lax.psum(both, "tensor")
-    low = both[:live_total].astype(BF16)
-    back = (lowrank_scale * both[live_total:]).astype(BF16)
+    both = rank_sums(tensor_count, both)
+    low = both[:, :live_total].astype(BF16)
+    back = (lowrank_scale * both[:, live_total:]).astype(BF16)
     fold_bf = fold.astype(BF16)
-    low_spread = jnp.where(picked, dot(low, fold_bf, 1, 1), 0.0).astype(BF16)
-    back_spread = jnp.where(picked, dot(back, fold_bf, 1, 1), 0.0).astype(BF16)
+    low_spread = jnp.where(picked, dot(low, fold_bf, 0, 1), 0.0).astype(BF16)
+    back_spread = jnp.where(picked, dot(back, fold_bf, 0, 1), 0.0).astype(BF16)
 
     through = through + dot(back_spread, down_all, 1, 0)
     grad_input = dot(place, through.astype(BF16), 0, 0).astype(BF16)

time: 267 us -> 243 us (0.910)
  blocking collectives: 46.3 us -> 11.8 us
  Pallas kernels: 147 us -> 160 us
    psum x1 -> x0, blocking collectives: 34.5 us -> none  [body(): both = lax.psum(both, 'tensor')]
    pallas_call x0 -> x1, Pallas kernels: none -> 9.97 us  [rank_sums(): pl.pallas_call(functools.partial(rank_kernel, count), in_specs=[vmem], ou...]
    pallas_call x1, Pallas kernels: 147 us -> 150 us  [base_products(): pl.pallas_call(functools.partial(base_kernel, count), in_specs=[vmem, vme...]
  transfers between devices with their start and end apart: 2 -> 2, of which waited for: 1 -> 1; matrix products, arithmetic and copies ran while one was open for 4% -> 4% of each run, Pallas kernels for 55% -> 62%
where the time goes in v3:
time: 243 us; the launch traced here: 242 us
  Pallas kernels  160 us (66%)
  waiting for transfers between devices  29.7 us (12%)
  matrix products  15.5 us (6%)
  starting transfers between devices  11.9 us (5%)
  blocking collectives  11.8 us (5%)
  local copies, waits for them, and re-layouts  9.68 us (4%)
    pallas_call x1, Pallas kernels, base_products(): pl.pallas_call(functools.partial(base_kernel, count), in_specs=[vmem, vme...  150 us
    all_to_all x1, waiting for transfers between devices, body(): lax.all_to_all(send, 'tensor', split_axis=0, concat_axis=0, tiled=True)  29.7 us
    dot_general x10, matrix products, dot(): lax.dot_general(a, b, (((ca,), (cb,)), ((), ())), preferred_element_type=...  15.1 us
    psum x1, blocking collectives, body(): own_grads = lax.psum(own_grads, 'dp').astype(BF16)  11.8 us
    pallas_call x1, Pallas kernels, rank_sums(): pl.pallas_call(functools.partial(rank_kernel, count), in_specs=[vmem], ou...  9.97 us
    all_to_all x1, starting transfers between devices, body(): lax.all_to_all(send, 'tensor', split_axis=0, concat_axis=0, tiled=True)  6.16 us
    all_to_all x1, starting transfers between devices, body(): lax.all_to_all(own_grads.reshape(tensor_count, own_rows, ff_dev + d_dev),...  5.7 us
  transfers between devices with their start and end apart: 2, of which 1 were waited for; matrix products, arithmetic and copies ran while one was open for 4% of the time, Pallas kernels for 62%

profile of v3, /device:TPU:28, one launch (start us, length us, event | category | flops | bytes accessed | tf_op | source)
XLA Modules:
  0.0 241.9 jit_solution(8587716625951110447)
XLA Ops:
  0.7 1.5 copy.25
  2.2 0.2 copy.24
  2.3 0.1 maximum_bitcast_fusion
  2.4 1.3 copy.21
  3.8 6.2 %all-to-all-start = ((bf16[8,32,2816]{2,1,0:T(8,128)(2,1)}), bf16[8,32,2816]{2,1,0:T(8,128)(2,1)}, u32[]{:S(2)}, u32[]{:S(2)}) async-start(bf16[8,32,2816]{2,1,0:T(8,128)(2,1)} %copy.21), calls=%async_computation | async-start | bytes 2883584 | tf_op jit(solution)/shard_map/all_to_all | solution.py:365
  9.9 0.1 select_reduce_fusion.1
  10.0 0.1 add_select_fusion
  10.2 0.1 select_reduce_fusion
  10.4 1.4 convolution_convert_fusion.3.grads_ref
  11.7 0.8 convolution_convert_fusion.1.acts_ref
  12.5 29.7 %all-to-all-done = bf16[8,32,2816]{2,1,0:T(8,128)(2,1)} async-done(((bf16[8,32,2816]{2,1,0:T(8,128)(2,1)}), bf16[8,32,2816]{2,1,0:T(8,128)(2,1)}, u32[]{:S(2)}, u32[]{:S(2)}) %all-to-all-start) | async-done | bytes 1441824 | tf_op jit(solution)/shard_map/all_to_all | solution.py:365
  42.2 1.6 convolution_select_fusion.2
  43.8 1.7 convolution_select_fusion.3
  45.5 0.5 fusion.8.part_ref
  45.9 10.0 %shard_map.103 = f32[16,640]{1,0:T(8,128)S(1)} custom-call(f32[16,640]{1,0:T(8,128)S(1)} %fusion.8.part_ref), custom_call_target="tpu_custom_call" | custom-call | tf_op jit(solution)/shard_map/pallas_call | solution.py:274
  55.9 0.3 fusion.3
  56.2 0.3 fusion.4
  56.5 0.5 convolution_multiply_fusion.1
  57.0 0.7 fusion.33
  57.7 1.8 pad_maximum_fusion
  59.5 11.8 %all-reduce.1 = bf16[256,2816]{1,0:T(8,128)(2,1)} all-reduce(f32[256,2816]{1,0:T(8,128)} %pad_maximum_fusion), channel_id=1, replica_groups=mesh['groups'=2,'dp'=2,'tensor'=8] {'dp'}, use_global_device_ids=true, to_apply=%region_2.3 | all-reduce | flops 720896 | bytes 4325376 | tf_op jit(solution)/shard_map/psum | solution.py:390
  71.3 5.7 %all-to-all-start.1 = ((bf16[8,32,2816]{2,1,0:T(8,128)(2,1)}), bf16[8,32,2816]{2,1,0:T(8,128)(2,1)}, u32[]{:S(2)}, u32[]{:S(2)}) async-start(bf16[8,32,2816]{2,1,0:T(8,128)(2,1)} %bitcast.32), calls=%async_computation.1 | async-start | bytes 2883584 | tf_op jit(solution)/shard_map/all_to_all | solution.py:391
  77.0 1.1 copy-done.2
  78.1 150.3 %shard_map.102 = (f32[320,1024]{1,0:T(8,128)}, f32[320,1792]{1,0:T(8,128)}) custom-call(bf16[320,1792]{1,0:T(8,128)(2,1)S(1)} %convolution_convert_fusion.1.acts_ref, bf16[320,1024]{1,0:T(8,128)(2,1)S(1)} %copy-done.2, bf16[1792,8192]{1,0:T(8,128)(2,1)} %w_ref.1), custom_call_target="tpu_custom_call" | custom-call | flops 18790481920 | bytes 146800640 | tf_op jit(solution)/shard_map/pallas_call | solution.py:296
  228.4 3.4 %convolution_convert_fusion.2 = bf16[512,1024]{1,0:T(8,128)(2,1)} fusion(f32[320,1024]{1,0:T(8,128)} %get-tuple-element.6, bf16[320,256]{1,0:T(8,128)(2,1)S(1)} %fusion.3, bf16[256,2816]{1,0:T(8,128)(2,1)} %bitcast.5, s32[512]{0:T(512)S(1)} %select_n.58), kind=kOutput, calls=%fused_computation.5 | convolution fusion | flops 504987648 | bytes 3049472 | tf_op jit(solution)/shard_map/dot_general | solution.py:18
  231.8 4.6 %convolution_convert_fusion = bf16[512,1792]{1,0:T(8,128)(2,1)} fusion(f32[320,1792]{1,0:T(8,128)} %get-tuple-element.7, bf16[320,256]{1,0:T(8,128)(2,1)S(1)} %fusion.4, bf16[256,2816]{1,0:T(8,128)(2,1)} %bitcast.5, s32[512]{0:T(512)S(1)} %select_n.58), kind=kOutput, calls=%fused_computation | convolution fusion | flops 883032064 | bytes 5212160 | tf_op jit(solution)/shard_map/dot_general | solution.py:18
  236.4 1.2 slice_bitcast_fusion
  237.6 0.5 copy.22
  238.1 1.3 reshape.90
  239.5 1.1 slice_bitcast_fusion.1
  240.6 0.3 copy.23
  240.9 1.0 reshape.91
  (17 shorter events, 0.1 us)
Async XLA Ops:
  0.6 11.1 %copy-start = (bf16[512,1792]{1,0:T(8,128)(2,1)S(1)}, bf16[512,1792]{1,0:T(8,128)(2,1)}, u32[]{:S(2)}) copy-start(bf16[512,1792]{1,0:T(8,128)(2,1)} %param.7) | copy-start | bytes 5505028
  0.6 1.5 copy-start.3
  3.8 6.2 %copy-start.4 = (s32[1,64]{1,0:T(1,128)S(1)}, s32[1,64]{1,0:T(1,128)}, u32[]{:S(2)}) copy-start(s32[1,64]{1,0:T(1,128)} %param.12) | copy-start | bytes 772
  3.8 6.5 %copy-start.5 = (s32[1,64]{1,0:T(1,128)S(1)}, s32[1,64]{1,0:T(1,128)}, u32[]{:S(2)}) copy-start(s32[1,64]{1,0:T(1,128)} %param.11) | copy-start | bytes 772
  3.8 6.6 %copy-start.6 = (bf16[512,1024]{1,0:T(8,128)(2,1)S(1)}, bf16[512,1024]{1,0:T(8,128)(2,1)}, u32[]{:S(2)}) copy-start(bf16[512,1024]{1,0:T(8,128)(2,1)} %param.13) | copy-start | bytes 3145732
  3.8 38.4 %all-to-all-start = ((bf16[8,32,2816]{2,1,0:T(8,128)(2,1)}), bf16[8,32,2816]{2,1,0:T(8,128)(2,1)}, u32[]{:S(2)}, u32[]{:S(2)}) async-start(bf16[8,32,2816]{2,1,0:T(8,128)(2,1)} %copy.21), calls=%async_computation | async-start | bytes 2883584 | tf_op jit(solution)/shard_map/all_to_all | solution.py:365
  45.5 11.0 %copy-start.1 = (bf16[320,1024]{1,0:T(8,128)(2,1)S(1)}, bf16[320,1024]{1,0:T(8,128)(2,1)}, u32[]{:S(2)}) copy-start(bf16[320,1024]{1,0:T(8,128)(2,1)} %convolution_convert_fusion.3.grads_ref) | copy-start | bytes 1966084
  71.3 165.1 %all-to-all-start.1 = ((bf16[8,32,2816]{2,1,0:T(8,128)(2,1)}), bf16[8,32,2816]{2,1,0:T(8,128)(2,1)}, u32[]{:S(2)}, u32[]{:S(2)}) async-start(bf16[8,32,2816]{2,1,0:T(8,128)(2,1)} %bitcast.32), calls=%async_computation.1 | async-start | bytes 2883584 | tf_op jit(solution)/shard_map/all_to_all | solution.py:391
  77.0 1.1 copy-start.2

commit v4 on v3

--- a/solution.py
+++ b/solution.py
@@ -108,6 +108,7 @@
         greet(ahead(k) * 2 + p)
 
     pl.semaphore_wait(barrier, lines)
+    near_copy().start()
 
     @pl.when(has_up)
     def _():
@@ -117,14 +118,14 @@
     def _():
         first_hop(down_send, q - 1).start()
 
+    gathered[me] = grads_ref[...]
+
     @pl.loop(0, lines)
     def _(k):
         w = weights(k)
         pair_out[k] = dot(acts_ref[...], w, 1, 0).astype(BF16)
         pair_copy(k).start()
 
-    near_copy().start()
-    gathered[me] = grads_ref[...]
 
     @pl.loop(0, lines)
     def _(k):

time: 243 us -> 242 us (level)
  no operation moved by 1% of the time
where the time goes in v4:
time: 242 us; the launch traced here: 241 us
  Pallas kernels  159 us (66%)
  waiting for transfers between devices  29.7 us (12%)
  matrix products  15.5 us (6%)
  starting transfers between devices  11.8 us (5%)
  blocking collectives  11.8 us (5%)
  local copies, waits for them, and re-layouts  9.68 us (4%)
    pallas_call x1, Pallas kernels, base_products(): pl.pallas_call(functools.partial(base_kernel, count), in_specs=[vmem, vme...  149 us
    all_to_all x1, waiting for transfers between devices, body(): lax.all_to_all(send, 'tensor', split_axis=0, concat_axis=0, tiled=True)  29.7 us
    dot_general x10, matrix products, dot(): lax.dot_general(a, b, (((ca,), (cb,)), ((), ())), preferred_element_type=...  15.1 us
    psum x1, blocking collectives, body(): own_grads = lax.psum(own_grads, 'dp').astype(BF16)  11.8 us
    pallas_call x1, Pallas kernels, rank_sums(): pl.pallas_call(functools.partial(rank_kernel, count), in_specs=[vmem], ou...  9.97 us
    all_to_all x1, starting transfers between devices, body(): lax.all_to_all(send, 'tensor', split_axis=0, concat_axis=0, tiled=True)  6.16 us
    all_to_all x1, starting transfers between devices, body(): lax.all_to_all(own_grads.reshape(tensor_count, own_rows, ff_dev + d_dev),...  5.69 us
  transfers between devices with their start and end apart: 2, of which 1 were waited for; matrix products, arithmetic and copies ran while one was open for 4% of the time, Pallas kernels for 62%

profile of v4, /device:TPU:28, one launch (start us, length us, event | category | flops | bytes accessed | tf_op | source)
XLA Modules:
  0.0 240.8 jit_solution(9709817830178480243)
XLA Ops:
  0.7 1.5 copy.25
  2.2 0.2 copy.24
  2.3 0.1 maximum_bitcast_fusion
  2.4 1.3 copy.21
  3.8 6.2 %all-to-all-start = ((bf16[8,32,2816]{2,1,0:T(8,128)(2,1)}), bf16[8,32,2816]{2,1,0:T(8,128)(2,1)}, u32[]{:S(2)}, u32[]{:S(2)}) async-start(bf16[8,32,2816]{2,1,0:T(8,128)(2,1)} %copy.21), calls=%async_computation | async-start | bytes 2883584 | tf_op jit(solution)/shard_map/all_to_all | solution.py:366
  9.9 0.1 select_reduce_fusion.1
  10.0 0.1 add_select_fusion
  10.2 0.1 select_reduce_fusion
  10.4 1.3 convolution_convert_fusion.3.grads_ref
  11.7 0.8 convolution_convert_fusion.1.acts_ref
  12.5 29.7 %all-to-all-done = bf16[8,32,2816]{2,1,0:T(8,128)(2,1)} async-done(((bf16[8,32,2816]{2,1,0:T(8,128)(2,1)}), bf16[8,32,2816]{2,1,0:T(8,128)(2,1)}, u32[]{:S(2)}, u32[]{:S(2)}) %all-to-all-start) | async-done | bytes 1441824 | tf_op jit(solution)/shard_map/all_to_all | solution.py:366
  42.2 1.6 convolution_select_fusion.2
  43.8 1.7 convolution_select_fusion.3
  45.5 0.5 fusion.8.part_ref
  45.9 10.0 %shard_map.103 = f32[16,640]{1,0:T(8,128)S(1)} custom-call(f32[16,640]{1,0:T(8,128)S(1)} %fusion.8.part_ref), custom_call_target="tpu_custom_call" | custom-call | tf_op jit(solution)/shard_map/pallas_call | solution.py:275
  55.9 0.3 fusion.3
  56.2 0.3 fusion.4
  56.5 0.5 convolution_multiply_fusion.1
  57.0 0.7 fusion.33
  57.7 1.8 pad_maximum_fusion
  59.5 11.8 %all-reduce.1 = bf16[256,2816]{1,0:T(8,128)(2,1)} all-reduce(f32[256,2816]{1,0:T(8,128)} %pad_maximum_fusion), channel_id=1, replica_groups=mesh['groups'=2,'dp'=2,'tensor'=8] {'dp'}, use_global_device_ids=true, to_apply=%region_2.3 | all-reduce | flops 720896 | bytes 4325376 | tf_op jit(solution)/shard_map/psum | solution.py:391
  71.3 5.7 %all-to-all-start.1 = ((bf16[8,32,2816]{2,1,0:T(8,128)(2,1)}), bf16[8,32,2816]{2,1,0:T(8,128)(2,1)}, u32[]{:S(2)}, u32[]{:S(2)}) async-start(bf16[8,32,2816]{2,1,0:T(8,128)(2,1)} %bitcast.32), calls=%async_computation.1 | async-start | bytes 2883584 | tf_op jit(solution)/shard_map/all_to_all | solution.py:392
  77.0 1.1 copy-done.2
  78.1 149.2 %shard_map.102 = (f32[320,1024]{1,0:T(8,128)}, f32[320,1792]{1,0:T(8,128)}) custom-call(bf16[320,1792]{1,0:T(8,128)(2,1)S(1)} %convolution_convert_fusion.1.acts_ref, bf16[320,1024]{1,0:T(8,128)(2,1)S(1)} %copy-done.2, bf16[1792,8192]{1,0:T(8,128)(2,1)} %w_ref.1), custom_call_target="tpu_custom_call" | custom-call | flops 18790481920 | bytes 146800640 | tf_op jit(solution)/shard_map/pallas_call | solution.py:297
  227.2 3.4 %convolution_convert_fusion.2 = bf16[512,1024]{1,0:T(8,128)(2,1)} fusion(f32[320,1024]{1,0:T(8,128)} %get-tuple-element.6, bf16[320,256]{1,0:T(8,128)(2,1)S(1)} %fusion.3, bf16[256,2816]{1,0:T(8,128)(2,1)} %bitcast.5, s32[512]{0:T(512)S(1)} %select_n.58), kind=kOutput, calls=%fused_computation.5 | convolution fusion | flops 504987648 | bytes 3049472 | tf_op jit(solution)/shard_map/dot_general | solution.py:18
  230.6 4.6 %convolution_convert_fusion = bf16[512,1792]{1,0:T(8,128)(2,1)} fusion(f32[320,1792]{1,0:T(8,128)} %get-tuple-element.7, bf16[320,256]{1,0:T(8,128)(2,1)S(1)} %fusion.4, bf16[256,2816]{1,0:T(8,128)(2,1)} %bitcast.5, s32[512]{0:T(512)S(1)} %select_n.58), kind=kOutput, calls=%fused_computation | convolution fusion | flops 883032064 | bytes 5212160 | tf_op jit(solution)/shard_map/dot_general | solution.py:18
  235.2 1.2 slice_bitcast_fusion
  236.5 0.5 copy.22
  237.0 1.3 reshape.90
  238.3 1.1 slice_bitcast_fusion.1
  239.4 0.3 copy.23
  239.7 1.0 reshape.91
  (17 shorter events, 0.1 us)
Async XLA Ops:
  0.6 11.1 %copy-start = (bf16[512,1792]{1,0:T(8,128)(2,1)S(1)}, bf16[512,1792]{1,0:T(8,128)(2,1)}, u32[]{:S(2)}) copy-start(bf16[512,1792]{1,0:T(8,128)(2,1)} %param.7) | copy-start | bytes 5505028
  0.6 1.5 copy-start.3
  3.8 6.2 %copy-start.4 = (s32[1,64]{1,0:T(1,128)S(1)}, s32[1,64]{1,0:T(1,128)}, u32[]{:S(2)}) copy-start(s32[1,64]{1,0:T(1,128)} %param.12) | copy-start | bytes 772
  3.8 6.5 %copy-start.5 = (s32[1,64]{1,0:T(1,128)S(1)}, s32[1,64]{1,0:T(1,128)}, u32[]{:S(2)}) copy-start(s32[1,64]{1,0:T(1,128)} %param.11) | copy-start | bytes 772
  3.8 6.6 %copy-start.6 = (bf16[512,1024]{1,0:T(8,128)(2,1)S(1)}, bf16[512,1024]{1,0:T(8,128)(2,1)}, u32[]{:S(2)}) copy-start(bf16[512,1024]{1,0:T(8,128)(2,1)} %param.13) | copy-start | bytes 3145732
  3.8 38.4 %all-to-all-start = ((bf16[8,32,2816]{2,1,0:T(8,128)(2,1)}), bf16[8,32,2816]{2,1,0:T(8,128)(2,1)}, u32[]{:S(2)}, u32[]{:S(2)}) async-start(bf16[8,32,2816]{2,1,0:T(8,128)(2,1)} %copy.21), calls=%async_computation | async-start | bytes 2883584 | tf_op jit(solution)/shard_map/all_to_all | solution.py:366
  45.5 11.0 %copy-start.1 = (bf16[320,1024]{1,0:T(8,128)(2,1)S(1)}, bf16[320,1024]{1,0:T(8,128)(2,1)}, u32[]{:S(2)}) copy-start(bf16[320,1024]{1,0:T(8,128)(2,1)} %convolution_convert_fusion.3.grads_ref) | copy-start | bytes 1966084
  71.3 163.9 %all-to-all-start.1 = ((bf16[8,32,2816]{2,1,0:T(8,128)(2,1)}), bf16[8,32,2816]{2,1,0:T(8,128)(2,1)}, u32[]{:S(2)}, u32[]{:S(2)}) async-start(bf16[8,32,2816]{2,1,0:T(8,128)(2,1)} %bitcast.32), calls=%async_computation.1 | async-start | bytes 2883584 | tf_op jit(solution)/shard_map/all_to_all | solution.py:392
  77.0 1.1 copy-start.2
